TPU v7x, 128 devices: a whole 4x4x4 slice. The times are simulated.
128 devices in a mesh: tm: 32 (over z, x, y_hi), mp: 4 (over y_lo, core).
Axes of the slice: x: 4, y: 4 (y_hi: 2, y_lo: 2; y = y_hi * 2 + y_lo), z: 4, core: 2. Of those that a mesh axis runs over, the one named last changes fastest.
Arguments:
- hidden: bfloat16 [128, 256, 3072], P('tm', None, 'mp'), may hold values from -6 to 6
- w_qkv: bfloat16 [3072, 3, 3072], P(None, None, 'mp'), may hold values from -0.109375 to 0.109375
- w_out: bfloat16 [3072, 3072], P('mp'), may hold values from -0.109375 to 0.109375
- modulation: float32 [50, 3, 3072], replicated, may hold values from -2 to 6
- levels: int32 [32], replicated, may hold values from 0 to 49, as said below
- counts: int32 [32], replicated, may hold values from 2 to 4, as said below
- entering: bfloat16 [4, 256, 3072], P(None, None, 'mp'), may hold values from -6 to 6
Outputs:
- advanced: bfloat16 [128, 256, 3072], P('tm', None, 'mp')
Inputs may be any that keep to these rules, and one draw needn't show every extreme that they name: levels start at 0 with the first span, never fall along the chain and end at 49 with the last span. The live frames of a span are its first counts slots; some span is full.
All inputs are finite; a program needn't handle non-finite values.
Results may differ from a plain program's by a relative error of at most 0.013.
The roundings to bfloat16 on the way count: a program that leaves them out, or rounds other values in their place, can miss the bound.
Values may be sent and summed in bfloat16 or wider, within the bound.
A program may use at most 256 MiB of HBM per device.

v0:
```python
import jax
import jax.numpy as jnp
from jax import lax
from jax.sharding import PartitionSpec as P

HD = 64
HALO = 2


def with_halo(shard, sides, width):
    for axis, dim in sides:
        size, length = (lax.axis_size(axis), shard.shape[dim])
        up = [(i, (i + 1) % size) for i in range(size - 1)]
        down = [(j, i) for i, j in up]
        last = lax.slice_in_dim(shard, length - width, length, axis=dim)
        initial = lax.slice_in_dim(shard, 0, width, axis=dim)
        before = lax.ppermute(last, axis, up)
        after = lax.ppermute(initial, axis, down)
        shard = jnp.concatenate([before, shard, after], axis=dim)
    return shard


def passed_along(value, axis, steps):
    count = lax.axis_size(axis)
    initial, last = (max(0, -steps), min(count, count - steps))
    return lax.ppermute(value, axis, [(source, source + steps) for source in range(initial, last)])


def layer_norm(rows):
    rows = rows.astype(jnp.float32)
    mean = jnp.mean(rows, axis=-1, keepdims=True)
    centred = rows - mean
    spread = jnp.mean(centred * centred, axis=-1, keepdims=True)
    return centred * lax.rsqrt(spread + 1e-06)


def per_device(hidden, w_qkv, w_out, modulation, levels, counts, entering):
    chain = lax.axis_size("tm")
    here = lax.axis_index("tm")
    frames, tokens, part_width = hidden.shape
    model_width = w_qkv.shape[0]
    head_cols = w_qkv.shape[2]
    local_heads = head_cols // HD
    rows = frames * tokens
    before = jnp.maximum(here - 1, 0)
    after = jnp.minimum(here + 1, chain - 1)
    own_mod = modulation[levels[here]]
    weight_all = w_qkv.reshape(model_width, 3 * head_cols)
    whole = lax.all_gather(hidden, "mp", axis=2, tiled=True)
    shaped = (layer_norm(whole) * (1.0 + own_mod[1]) + own_mod[0]).astype(jnp.bfloat16)
    proj = jnp.dot(
        shaped.reshape(rows, model_width), weight_all, preferred_element_type=jnp.float32
    )
    proj = proj.astype(jnp.bfloat16).reshape(frames, tokens, 3, head_cols)
    query = proj[:, :, 0]
    pairs = with_halo(proj[:, :, 1:], (("tm", 0),), HALO)
    slots = jnp.arange(frames + 2 * HALO, dtype=jnp.int32)
    prev_ok = (slots < HALO) & (here > 0) & (frames - HALO + slots < counts[before])
    own_ok = (slots >= HALO) & (slots < HALO + frames) & (slots - HALO < counts[here])
    next_ok = (
        (slots >= HALO + frames) & (here < chain - 1) & (slots - HALO - frames < counts[after])
    )
    live = jnp.broadcast_to(
        (prev_ok | own_ok | next_ok)[:, None], (frames + 2 * HALO, tokens)
    ).reshape(-1)
    keys = pairs[:, :, 0].reshape(-1, local_heads, HD)
    values = pairs[:, :, 1].reshape(-1, local_heads, HD)
    queries = query.reshape(rows, local_heads, HD)
    scores = jnp.einsum("qhd,khd->hqk", queries, keys, preferred_element_type=jnp.float32) * HD ** (
        -0.5
    )
    scores = jnp.where(live[None, None, :], scores, -1e30)
    top = jnp.max(scores, axis=-1, keepdims=True)
    expd = jnp.exp(scores - top)
    weights = (expd / jnp.sum(expd, axis=-1, keepdims=True)).astype(jnp.bfloat16)
    attended = jnp.einsum("hqk,khd->qhd", weights, values, preferred_element_type=jnp.float32)
    attended = attended.astype(jnp.bfloat16).reshape(rows, head_cols)
    partial_terms = jnp.dot(attended, w_out, preferred_element_type=jnp.float32).reshape(
        frames, tokens, model_width
    )
    mixed = lax.psum_scatter(
        partial_terms.astype(jnp.bfloat16), "mp", scatter_dimension=2, tiled=True
    ).astype(jnp.float32)
    gate = lax.dynamic_slice_in_dim(own_mod[2], lax.axis_index("mp") * part_width, part_width, 0)
    stepped = (hidden.astype(jnp.float32) + gate * mixed).astype(jnp.bfloat16)
    moved = passed_along(stepped, "tm", -1)
    return jnp.where(here == chain - 1, entering, moved)


def solution(mesh):
    in_specs = (
        P("tm", None, "mp"),
        P(None, None, "mp"),
        P("mp", None),
        P(),
        P(),
        P(),
        P(None, None, "mp"),
    )
    out_specs = P("tm", None, "mp")
    return jax.shard_map(
        per_device, mesh=mesh, in_specs=in_specs, out_specs=out_specs, check_vma=False
    )
```

profile of v0, /device:TPU:1, one launch (start us, length us, event | category | flops | bytes accessed | tf_op | source)
XLA Modules:
  0.0 421.3 jit_solution(9065977526222381540)
XLA Ops:
  6.5 0.0 all-gather.2.cloned.1.call-start
  6.5 0.7 all-gather.2.cloned.1.call-update
  7.3 0.0 reduce-scatter.2.cloned.1.call-start
  7.3 1.2 dynamic_slice.18
  9.8 18.8 %copy.12 = bf16[3072,3,768]{0,2,1:T(8,128)(2,1)} copy(bf16[3072,3,768]{2,0,1:T(8,128)(2,1)} %param.8) | data formatting | bytes 28311552 | tf_op args[1]
  29.3 1.0 dynamic-slice_add_fusion
  30.3 46.4 %all-gather.2.cloned.1.call-done = bf16[4,256,3072]{2,1,0:T(8,128)(2,1)} async-done(((bf16[4,256,768]{2,1,0:T(8,128)(2,1)}), bf16[4,256,3072]{2,1,0:T(8,128)(2,1)}) %all-gather.2.cloned.1.call-update) | async-done | bytes 6291472 | tf_op jit(solution)/shard_map/all_gather | solution.py:49
  76.7 0.0 copy-start
  76.7 3.8 convert_reduce_fusion
  80.5 0.8 copy-done
  81.2 1.8 fusion.8
  83.0 3.9 fusion.11
  86.9 19.0 %convolution_convert_fusion.1 = bf16[1024,2304]{1,0:T(8,128)(2,1)} fusion(bf16[1024,3072]{1,0:T(8,128)(2,1)S(1)} %bitcast.35, bf16[3072,2304]{0,1:T(8,128)(2,1)} %bitcast.34), kind=kOutput, calls=%fused_computation.20 | convolution fusion | flops 14497873920 | bytes 25165824 | tf_op jit(solution)/shard_map/dot_general | solution.py:51
  105.9 6.7 %copy.13 = bf16[1024,2304]{0,1:T(8,128)(2,1)} copy(bf16[1024,2304]{1,0:T(8,128)(2,1)} %convolution_convert_fusion.1) | data formatting | bytes 9437184 | tf_op jit(solution)/shard_map/convert_element_type | solution.py:54
  112.6 8.9 %reshape.65 = bf16[4,256,3,768]{1,0,3,2:T(4,128)(2,1)} reshape(bf16[1024,2304]{0,1:T(8,128)(2,1)} %copy.13) | data formatting | bytes 9437184 | tf_op jit(solution)/shard_map/reshape | solution.py:54
  121.5 0.0 copy-start.4
  121.5 6.6 %fusion.21 = (bf16[2,256,2,768]{1,0,3,2:T(2,128)(2,1)}, bf16[2,256,2,768]{1,0,3,2:T(2,128)(2,1)}) fusion(bf16[4,256,3,768]{1,0,3,2:T(4,128)(2,1)} %reshape.65), kind=kLoop, calls=%fused_computation.36 | loop fusion | bytes 6291456 | tf_op jit(solution)/shard_map/slice | solution.py:15
  128.1 1.3 collective-permute-start.1
  129.4 6.7 %collective-permute-start = (bf16[2,256,2,768]{1,0,3,2:T(2,128)(2,1)}, bf16[2,256,2,768]{1,0,3,2:T(2,128)(2,1)}, u32[]{:S(2)}, u32[]{:S(2)}) collective-permute-start(bf16[2,256,2,768]{1,0,3,2:T(2,128)(2,1)} %get-tuple-element.7), channel_id=1, source_target_pairs={{0,4},{4,8},{8,12},{12,16},{16,20},{20,24},{24,28},{28,32},{32,36}... | collective-permute-start | bytes 4718600 | tf_op jit(solution)/shard_map/ppermute | solution.py:17
  136.1 0.0 copy-done.4
  136.1 0.6 fusion.22
  136.7 1.9 and_or_fusion
  138.6 0.1 broadcast_in_dim.16
  138.7 0.0 slice-start
  138.7 4.8 %slice.42 = bf16[4,256,2,768]{1,0,3,2:T(4,128)(2,1)} slice(bf16[4,256,3,768]{1,0,3,2:T(4,128)(2,1)} %reshape.65), slice={[0:4], [0:256], [1:3], [0:768]} | slice | bytes 6291456 | tf_op jit(solution)/shard_map/slice | solution.py:56
  143.5 0.0 slice-done
  143.5 2.3 reshape_squeeze.10
  145.8 55.6 %collective-permute-done.1 = bf16[2,256,2,768]{1,0,3,2:T(2,128)(2,1)S(1)} collective-permute-done((bf16[2,256,2,768]{1,0,3,2:T(2,128)(2,1)}, bf16[2,256,2,768]{1,0,3,2:T(2,128)(2,1)S(1)}, u32[]{:S(2)}, u32[]{:S(2)}) %collective-permute-start.1) | collective-permute-done | bytes 1572896 | tf_op jit(solution)/shard_map/ppermute | solution.py:18
  201.5 0.0 collective-permute-done
  201.5 6.5 %pad_maximum_fusion = bf16[8,256,2,768]{1,0,3,2:T(8,128)(2,1)S(1)} fusion(bf16[2,256,2,768]{1,0,3,2:T(2,128)(2,1)S(1)} %collective-permute-done.1, bf16[4,256,2,768]{1,0,3,2:T(4,128)(2,1)} %slice.42, bf16[2,256,2,768]{1,0,3,2:T(2,128)(2,1)} %collective-permute-done), kind=kLoop, calls=%fused_computation.18 | loop fusion | flops 18874368 | bytes 12582912 | tf_op jit(solution)/shard_map/concatenate | solution.py:19
  208.0 2.1 fusion.20
  210.0 5.9 %reshape_squeeze.9 = bf16[2048,12,64]{0,2,1:T(8,128)(2,1)} reshape(bf16[8,256,1,768]{1,0,3,2:T(8,128)(2,1)} %get-tuple-element.6) | data formatting | bytes 6291456 | tf_op jit(solution)/shard_map/reshape;squeeze | solution.py:67
  215.9 3.4 reshape_squeeze.11
  219.3 0.0 copy-start.2
  219.3 39.6 %fusion.23 = (f32[12,1024]{1,0:T(8,128)S(1)}, f32[12,1024,2048]{2,1,0:T(8,128)}) fusion(pred[2048]{0:T(1024)(128)(4,1)S(1)} %broadcast_in_dim.17, bf16[1024,12,64]{0,2,1:T(8,128)(2,1)} %reshape_squeeze.10, bf16[2048,12,64]{0,2,1:T(8,128)(2,1)} %reshape_squeeze.11), kind=kOutput, calls=%fused_computation.38 | convolution fusion | flops 3321890816 | bytes 105433088 | tf_op jit(solution)/shard_map/sub | solution.py:74
  258.9 0.0 copy-done.2
  258.9 33.9 %fusion.17 = bf16[1024,12,64]{0,2,1:T(8,128)(2,1)} fusion(bf16[2048,12,64]{0,2,1:T(8,128)(2,1)S(1)} %copy-done.2, f32[12,1024,2048]{2,1,0:T(8,128)} %get-tuple-element.15, f32[12,1024]{1,0:T(8,128)S(1)} %get-tuple-element.14), kind=kOutput, calls=%fused_computation.26 | convolution fusion | flops 3272343552 | bytes 105431040 | tf_op jit(solution)/shard_map/hqk,khd->qhd/dot_general | solution.py:76
  292.7 2.9 dot_general.17
  295.6 9.6 %convolution_convert_fusion = bf16[4,256,3072]{2,1,0:T(8,128)(2,1)} fusion(bf16[768,3072]{1,0:T(8,128)(2,1)} %param.9, bf16[4,256,768]{1,0,2:T(4,128)(2,1)S(1)} %dot_general.17), kind=kOutput, calls=%fused_computation.19 | convolution fusion | flops 4834983936 | bytes 12582912 | tf_op jit(solution)/shard_map/dot_general | solution.py:78
  305.2 0.0 reduce-scatter.2.cloned.1.call-update
  305.3 1.0 dynamic-slice_reduce_fusion
  306.3 64.7 %reduce-scatter.2.cloned.1.call-done = bf16[4,256,768]{2,1,0:T(8,128)(2,1)} async-done(((bf16[4,256,3072]{2,1,0:T(8,128)(2,1)}), bf16[4,256,768]{2,1,0:T(8,128)(2,1)}) %reduce-scatter.2.cloned.1.call-update) | async-done | bytes 1572880 | tf_op jit(solution)/shard_map/reduce_scatter | solution.py:81
  371.0 0.0 copy-done.1
  371.0 3.0 add_convert_fusion
  374.0 1.3 collective-permute-start.2
  375.3 37.9 %collective-permute-done.2 = bf16[4,256,768]{2,1,0:T(8,128)(2,1)S(1)} collective-permute-done((bf16[4,256,768]{2,1,0:T(8,128)(2,1)}, bf16[4,256,768]{2,1,0:T(8,128)(2,1)S(1)}, u32[]{:S(2)}, u32[]{:S(2)}) %collective-permute-start.2) | collective-permute-done | bytes 1572896 | tf_op jit(solution)/shard_map/ppermute | solution.py:26
  413.1 0.0 copy-done.3
  413.1 1.3 broadcast_select_fusion
  (5 shorter events, 0.0 us)
Async XLA Ops:
  6.5 70.1 %all-gather.2.cloned.1.call-start = ((), (), s32[]{:S(2)}) async-start(), calls=%async_computation.1 | async-start | bytes 7864320 | tf_op jit(solution)/shard_map/all_gather | solution.py:49
  7.3 363.7 %reduce-scatter.2.cloned.1.call-start = ((), (), s32[]{:S(2)}) async-start(), calls=%async_computation.2 | async-start | bytes 7864320 | tf_op jit(solution)/shard_map/reduce_scatter | solution.py:81
  76.7 4.6 %copy-start = (bf16[4,256,3072]{2,1,0:T(8,128)(2,1)S(1)}, bf16[4,256,3072]{2,1,0:T(8,128)(2,1)}, u32[]{:S(2)}) copy-start(bf16[4,256,3072]{2,1,0:T(8,128)(2,1)} %all-gather.2.cloned.1.call-done) | copy-start | bytes 18874372
  121.5 14.6 %copy-start.4 = (s32[32]{0:T(128)S(1)}, s32[32]{0:T(128)}, u32[]{:S(2)}) copy-start(s32[32]{0:T(128)} %param.12) | copy-start | bytes 388
  128.1 73.3 %collective-permute-start.1 = (bf16[2,256,2,768]{1,0,3,2:T(2,128)(2,1)}, bf16[2,256,2,768]{1,0,3,2:T(2,128)(2,1)S(1)}, u32[]{:S(2)}, u32[]{:S(2)}) collective-permute-start(bf16[2,256,2,768]{1,0,3,2:T(2,128)(2,1)} %get-tuple-element.8), channel_id=1, source_target_pairs={{4,0},{8,4},{12,8},{16,12},{20,16},{24,20},{28,24},{32,28},{36,32}... | collective-permute-start | bytes 4718600 | tf_op jit(solution)/shard_map/ppermute | solution.py:18
  129.4 72.1 %collective-permute-start = (bf16[2,256,2,768]{1,0,3,2:T(2,128)(2,1)}, bf16[2,256,2,768]{1,0,3,2:T(2,128)(2,1)}, u32[]{:S(2)}, u32[]{:S(2)}) collective-permute-start(bf16[2,256,2,768]{1,0,3,2:T(2,128)(2,1)} %get-tuple-element.7), channel_id=1, source_target_pairs={{0,4},{4,8},{8,12},{12,16},{16,20},{20,24},{24,28},{28,32},{32,36}... | collective-permute-start | bytes 4718600 | tf_op jit(solution)/shard_map/ppermute | solution.py:17
  138.7 4.8 %slice-start = ((bf16[4,256,3,768]{1,0,3,2:T(4,128)(2,1)}), bf16[4,256,1,768]{1,0,3,2:T(4,128)(2,1)S(1)}, s32[]{:S(2)}) async-start(bf16[4,256,3,768]{1,0,3,2:T(4,128)(2,1)} %reshape.65), calls=%async_computation.3 | async-start | bytes 3145728 | tf_op jit(solution)/shard_map/slice | solution.py:55
  219.3 39.6 %copy-start.2 = (bf16[2048,12,64]{0,2,1:T(8,128)(2,1)S(1)}, bf16[2048,12,64]{0,2,1:T(8,128)(2,1)}, u32[]{:S(2)}) copy-start(bf16[2048,12,64]{0,2,1:T(8,128)(2,1)} %reshape_squeeze.9) | copy-start | bytes 9437188
  305.2 65.7 %copy-start.1 = (bf16[4,256,768]{2,1,0:T(8,128)(2,1)S(1)}, bf16[4,256,768]{2,1,0:T(8,128)(2,1)}, u32[]{:S(2)}) copy-start(bf16[4,256,768]{2,1,0:T(8,128)(2,1)} %param.7) | copy-start | bytes 4718596
  305.2 107.9 %copy-start.3 = (bf16[4,256,768]{2,1,0:T(8,128)(2,1)S(1)}, bf16[4,256,768]{2,1,0:T(8,128)(2,1)}, u32[]{:S(2)}) copy-start(bf16[4,256,768]{2,1,0:T(8,128)(2,1)} %param.13) | copy-start | bytes 4718596
  374.0 39.2 %collective-permute-start.2 = (bf16[4,256,768]{2,1,0:T(8,128)(2,1)}, bf16[4,256,768]{2,1,0:T(8,128)(2,1)S(1)}, u32[]{:S(2)}, u32[]{:S(2)}) collective-permute-start(bf16[4,256,768]{2,1,0:T(8,128)(2,1)} %add_convert_fusion), channel_id=1, source_target_pairs={{4,0},{8,4},{12,8},{16,12},{20,16},{24,20},{28,24},{32,28},{36,32}... | collective-permute-start | bytes 4718600 | tf_op jit(solution)/shard_map/ppermute | solution.py:26
Sparse Core Ops, SparseCore 0:
  9.0 67.5 all-gather.1
  305.4 65.5 reduce-scatter.1
where the time goes:
time: 425 us; the launch traced here: 421 us
  waiting for transfers between devices  205 us (48%)
  matrix products  102 us (24%)
  local copies, waits for them, and re-layouts  66 us (16%)
  other arithmetic  23.2 us (5%)
  between operations  15.4 us (4%)
  starting transfers between devices  9.27 us (2%)
    reduce_scatter x1, waiting for transfers between devices, per_device(): lax.psum_scatter(partial_terms.astype(jnp.bfloat16), 'mp', scatter_dimens...  64.7 us
    ppermute x1, waiting for transfers between devices, with_halo(): after = lax.ppermute(initial, axis, down)  55.6 us
    all_gather x1, waiting for transfers between devices, per_device(): whole = lax.all_gather(hidden, 'mp', axis=2, tiled=True)  46.4 us
    sub x1, matrix products, per_device(): expd = jnp.exp(scores - top)  39.6 us
    ppermute x1, waiting for transfers between devices, passed_along(): lax.ppermute(value, axis, [(source, source + steps) for source in range(i...  37.9 us
    dot_general x1, matrix products, per_device(): jnp.einsum('hqk,khd->qhd', weights, values, preferred_element_type=jnp.fl...  33.9 us
    unnamed x11, local copies, waits for them, and re-layouts  19.6 us
    dot_general x1, matrix products, per_device(): jnp.dot(shaped.reshape(rows, model_width), weight_all, preferred_element_...  19 us
  transfers between devices with their start and end apart: 5, of which 4 were waited for; matrix products, arithmetic and copies ran while one was open for 8% of the time, Pallas kernels for 0%

commit v1 on v0

v1 whole, which is shorter than its diff:
```python
import functools

import jax
import jax.numpy as jnp
from jax import lax
from jax.experimental import pallas as pl
from jax.experimental.pallas import tpu as pltpu
from jax.sharding import PartitionSpec as P

HD = 64
HALO = 2
QUAD = 256
LN_ROWS = 32
MESH = pl.DeviceIdType.MESH

OWN_CORE, OWN_Y, OWN_FWD = 0, 4, 8
N_OWN, N_FWD, N_CORE_A, N_CORE_B = 12, 14, 16, 18
P_OWN, P_Y, P_CORE_A, P_CORE_B = 20, 22, 24, 26
TERM, PRE, FIN = 28, 32, 36
N_SEM = 40


def kernel(
    chain, hid, w, w_out, mods, gate, live, out,
    x, wv, wo, shaped, qb, kb, vb, vlive, att, tsib, rsib, town, pre, rpre, fin,
    send_sem, recv_sem, w_sem, local_sem,
):
    c = lax.axis_index("tm")
    m = lax.axis_index("mp")
    sib, par, dia = m ^ 1, m ^ 2, m ^ 3
    up = lax.rem(c + 1, chain)
    down = lax.rem(c + chain - 1, chain)
    frames, tokens, part = hid.shape
    width = 4 * part
    keys = (frames + 2 * HALO) * tokens
    to_sib, to_par = (c, sib), (c, par)
    to_up, to_down = (up, par), (down, par)

    def rc(src, dst, s, dev):
        return pltpu.make_async_remote_copy(
            src_ref=src, dst_ref=dst, send_sem=send_sem.at[s], recv_sem=recv_sem.at[s],
            device_id=dev, device_id_type=MESH,
        )

    def arrived(dst, s):
        rc(dst, dst, s, to_sib).wait_recv()

    def w_copy(j):
        return pltpu.make_async_copy(
            w.at[j // 3, :, pl.ds((j % 3) * QUAD, QUAD)], wv.at[j], w_sem.at[j]
        )

    def wo_copy(g):
        return pltpu.make_async_copy(w_out.at[:, pl.ds(g * part, part)], wo.at[g], w_sem.at[9 + g])

    own_copy = pltpu.make_async_copy(hid, x.at[m, pl.ds(HALO, frames)], local_sem)
    own_copy.start()
    for j in range(9):
        w_copy(j).start()
    for g in range(4):
        wo_copy(g).start()

    barrier = pltpu.get_barrier_semaphore()
    for dev in (to_sib, to_par, to_up, to_down):
        pl.semaphore_signal(barrier, inc=1, device_id=dev, device_id_type=MESH)
    pl.semaphore_wait(barrier, 4)

    def own_core(i):
        return rc(hid.at[i], x.at[m, HALO + i], OWN_CORE + i, to_sib)

    def own_y(i):
        return rc(hid.at[i], x.at[m, HALO + i], OWN_Y + i, to_par)

    def own_fwd(i):
        return rc(x.at[par, HALO + i], x.at[par, HALO + i], OWN_FWD + i, to_sib)

    def n_own(i):
        return rc(hid.at[i], x.at[m, HALO + frames + i], N_OWN + i, to_down)

    def n_fwd(i):
        return rc(x.at[par, HALO + i], x.at[par, HALO + frames + i], N_FWD + i, to_down)

    def n_core_a(i):
        s = HALO + frames + i
        return rc(x.at[par, s], x.at[par, s], N_CORE_A + i, to_sib)

    def n_core_b(i):
        s = HALO + frames + i
        return rc(x.at[m, s], x.at[m, s], N_CORE_B + i, to_sib)

    def p_own(i):
        return rc(hid.at[frames - HALO + i], x.at[m, i], P_OWN + i, to_up)

    def p_y(i):
        return rc(x.at[par, i], x.at[par, i], P_Y + i, to_par)

    def p_core_a(i):
        return rc(x.at[par, i], x.at[par, i], P_CORE_A + i, to_sib)

    def p_core_b(i):
        return rc(x.at[m, i], x.at[m, i], P_CORE_B + i, to_sib)

    for i in range(frames):
        own_y(i).start()
        own_core(i).start()
    for i in range(HALO):
        n_own(i).start()
        p_own(i).start()
    for i in range(keys // tokens):
        vlive[pl.ds(i * tokens, tokens), :] = jnp.broadcast_to(
            live[i:i + 1, :], (tokens, 128)
        ).astype(jnp.bfloat16)
    own_copy.wait()

    def project(slot, span):
        def norm(b, carry):
            rows = pl.ds(pl.multiple_of(b * LN_ROWS, LN_ROWS), LN_ROWS)
            xs = [x[f, slot, rows, :].astype(jnp.float32) for f in range(4)]
            mean = sum(jnp.sum(v, axis=1, keepdims=True) for v in xs) * (1.0 / width)
            xs = [v - mean for v in xs]
            var = sum(jnp.sum(v * v, axis=1, keepdims=True) for v in xs) * (1.0 / width)
            r = lax.rsqrt(var + 1e-06)
            for f in range(4):
                cols = slice(f * part, (f + 1) * part)
                y = xs[f] * r * mods[span, 1:2, cols] + mods[span, 0:1, cols]
                shaped[rows, cols] = y.astype(jnp.bfloat16)
            return carry

        lax.fori_loop(0, tokens // LN_ROWS, norm, 0)
        lv = live[pl.ds(slot, 1), :]
        lv = jnp.concatenate([lv, lv], axis=1)
        rows = pl.ds(pl.multiple_of(slot * tokens, tokens), tokens)
        first = pl.ds(HALO * tokens, tokens)

        def tile(t, carry):
            k = jnp.dot(shaped[...], wv[3 + t], preferred_element_type=jnp.float32)
            kb[t, rows, :] = k.astype(jnp.bfloat16)
            k0 = kb[t, first, :].astype(jnp.float32)
            kb[t, rows, :] = jnp.where(lv > 0.5, k, k0).astype(jnp.bfloat16)
            v = jnp.dot(shaped[...], wv[6 + t], preferred_element_type=jnp.float32)
            vb[t, rows, :] = jnp.where(lv > 0.5, v, 0.0).astype(jnp.bfloat16)
            return carry

        lax.fori_loop(0, 3, tile, 0)

    def project_query(i):
        rows = pl.ds(pl.multiple_of(i * tokens, tokens), tokens)

        def tile(t, carry):
            q = jnp.dot(shaped[...], wv[t], preferred_element_type=jnp.float32)
            q = q.astype(jnp.bfloat16).astype(jnp.float32) * HD ** (-0.5)
            qb[t, rows, :] = q.astype(jnp.bfloat16)
            return carry

        lax.fori_loop(0, 3, tile, 0)

    for j in range(9):
        w_copy(j).wait()

    def gather_step(j, carry):
        slot = lax.rem(j + HALO, frames + 2 * HALO)
        span = jnp.where(j < frames, 1, jnp.where(j < frames + HALO, 2, 0))

        @pl.when(j < frames)
        def _():
            arrived(x.at[par, HALO + j], OWN_Y + j)
            own_fwd(j).start()

            @pl.when(j < HALO)
            def _():
                n_fwd(j).start()

            arrived(x.at[sib, HALO + j], OWN_CORE + j)
            arrived(x.at[dia, HALO + j], OWN_FWD + j)

        @pl.when((j >= frames) & (j < frames + HALO))
        def _():
            i = j - frames
            arrived(x.at[m, slot], N_FWD + i)
            n_core_b(i).start()
            arrived(x.at[dia, slot], N_CORE_A + i)
            arrived(x.at[sib, slot], N_CORE_B + i)

        @pl.when(j >= frames + HALO)
        def _():
            i = j - frames - HALO
            arrived(x.at[m, slot], P_Y + i)
            p_core_b(i).start()
            arrived(x.at[dia, slot], P_CORE_A + i)
            arrived(x.at[sib, slot], P_CORE_B + i)

        project(slot, span)

        @pl.when(j < frames)
        def _():
            project_query(j)

        @pl.when(j == frames - 1)
        def _():
            for i in range(HALO):
                arrived(x.at[par, i], P_OWN + i)
                p_y(i).start()
                p_core_a(i).start()
            for i in range(HALO):
                arrived(x.at[par, HALO + frames + i], N_OWN + i)
                n_core_a(i).start()

        return carry

    lax.fori_loop(0, frames + 2 * HALO, gather_step, 0)

    for g in range(4):
        wo_copy(g).wait()

    lane = lax.broadcasted_iota(jnp.int32, (1, 128), 1)
    low = lane < HD

    def attend(i):
        rows = pl.ds(pl.multiple_of(i * tokens, tokens), tokens)

        def pair(n, carry):
            t = n // 2
            for h2 in range(1):
                cols = pl.ds(pl.multiple_of((n % 2) * 128, 128), 128)
                q = qb[t, rows, cols]
                k = kb[t, :, cols]
                v = jnp.concatenate([vb[t, :, cols], vlive[...]], axis=1)
                parts = []
                for side in (low, ~low):
                    qm = jnp.where(side, q, jnp.zeros_like(q))
                    s = lax.dot_general(
                        qm, k, (((1,), (1,)), ((), ())), preferred_element_type=jnp.float32
                    )
                    top = jnp.max(s, axis=1, keepdims=True)
                    p = jnp.exp(s - top).astype(jnp.bfloat16)
                    o = jnp.dot(p, v, preferred_element_type=jnp.float32)
                    parts.append(o[:, :128] / o[:, 128:])
                att[n] = jnp.where(low, parts[0], parts[1]).astype(jnp.bfloat16)
            return carry

        lax.fori_loop(0, 6, pair, 0)

    def term(g):
        a = jnp.concatenate([att[n] for n in range(6)], axis=1)
        return jnp.dot(a, wo[g], preferred_element_type=jnp.float32).astype(jnp.bfloat16)

    def term_copy(i):
        return rc(tsib.at[i % 2], rsib.at[i], TERM + i, to_sib)

    def pre_copy(i):
        return rc(pre.at[i % 2], rpre.at[i], PRE + i, to_par)

    def fin_copy(i):
        return rc(fin.at[i % 2], out.at[i], FIN + i, to_down)

    def finish(i):
        slot = i % 2

        @pl.when(i >= 2)
        def _():
            fin_copy(i - 2).wait_send()

        arrived(rpre.at[i], PRE + i)
        mixed = (
            town[slot, 1].astype(jnp.float32)
            + rsib[i, 1].astype(jnp.float32)
            + rpre[i].astype(jnp.float32)
        )
        res = x[par, HALO + i].astype(jnp.float32) + gate[par] * mixed
        fin[slot] = res.astype(jnp.bfloat16)
        fin_copy(i).start()

    def frame(i, carry):
        slot = i % 2
        attend(i)

        @pl.when(i >= 2)
        def _():
            term_copy(i - 2).wait_send()
            pre_copy(i - 2).wait_send()

        tsib[slot, 0] = term(sib)
        tsib[slot, 1] = term(dia)
        term_copy(i).start()
        town[slot, 0] = term(m)
        town[slot, 1] = term(par)
        arrived(rsib.at[i], TERM + i)
        pre[slot] = (town[slot, 0].astype(jnp.float32) + rsib[i, 0].astype(jnp.float32)).astype(
            jnp.bfloat16
        )
        pre_copy(i).start()

        @pl.when(i >= 1)
        def _():
            finish(i - 1)

        return carry

    lax.fori_loop(0, frames, frame, 0)
    finish(frames - 1)

    for i in range(frames):
        own_y(i).wait_send()
        own_core(i).wait_send()
        own_fwd(i).wait_send()
        arrived(out.at[i], FIN + i)
    for i in range(HALO):
        for cp in (n_own, n_fwd, n_core_a, n_core_b, p_own, p_y, p_core_a, p_core_b):
            cp(i).wait_send()
    for i in range(frames - 2, frames):
        term_copy(i).wait_send()
        pre_copy(i).wait_send()
        fin_copy(i).wait_send()


def per_device(hidden, w_qkv, w_out, modulation, levels, counts, entering):
    chain = lax.axis_size("tm")
    here = lax.axis_index("tm")
    frames, tokens, part = hidden.shape
    model = w_qkv.shape[0]
    heads_w = w_qkv.shape[2]
    before = jnp.maximum(here - 1, 0)
    after = jnp.minimum(here + 1, chain - 1)
    slots = jnp.arange(frames + 2 * HALO, dtype=jnp.int32)
    prev_ok = (slots < HALO) & (here > 0) & (frames - HALO + slots < counts[before])
    own_ok = (slots >= HALO) & (slots < HALO + frames) & (slots - HALO < counts[here])
    next_ok = (
        (slots >= HALO + frames) & (here < chain - 1) & (slots - HALO - frames < counts[after])
    )
    live = jnp.broadcast_to(
        (prev_ok | own_ok | next_ok).astype(jnp.float32)[:, None], (frames + 2 * HALO, 128)
    )
    near = modulation[levels[jnp.stack([before, here, after])]]
    mods = jnp.stack([near[:, 0], 1.0 + near[:, 1]], axis=1)
    gate = near[1, 2].reshape(4, 1, part)
    n_keys = (frames + 2 * HALO) * tokens
    bf = jnp.bfloat16
    vmem = pl.BlockSpec(memory_space=pltpu.VMEM)
    hbm = pl.BlockSpec(memory_space=pl.ANY)
    moved = pl.pallas_call(
        functools.partial(kernel, chain),
        out_shape=jax.ShapeDtypeStruct((frames, tokens, part), bf),
        in_specs=[hbm, hbm, hbm, vmem, vmem, vmem],
        out_specs=hbm,
        scratch_shapes=[
            pltpu.VMEM((4, frames + 2 * HALO, tokens, part), bf),
            pltpu.VMEM((9, model, QUAD), bf),
            pltpu.VMEM((4, heads_w, part), bf),
            pltpu.VMEM((tokens, model), bf),
            pltpu.VMEM((3, frames * tokens, QUAD), bf),
            pltpu.VMEM((3, n_keys, QUAD), bf),
            pltpu.VMEM((3, n_keys, QUAD), bf),
            pltpu.VMEM((n_keys, 128), bf),
            pltpu.VMEM((6, tokens, 128), bf),
            pltpu.VMEM((2, 2, tokens, part), bf),
            pltpu.VMEM((frames, 2, tokens, part), bf),
            pltpu.VMEM((2, 2, tokens, part), bf),
            pltpu.VMEM((2, tokens, part), bf),
            pltpu.VMEM((frames, tokens, part), bf),
            pltpu.VMEM((2, tokens, part), bf),
            pltpu.SemaphoreType.DMA((N_SEM,)),
            pltpu.SemaphoreType.DMA((N_SEM,)),
            pltpu.SemaphoreType.DMA((13,)),
            pltpu.SemaphoreType.DMA,
        ],
        compiler_params=pltpu.CompilerParams(
            collective_id=0, has_side_effects=True, vmem_limit_bytes=63 * 1000 * 1000
        ),
        cost_estimate=pl.CostEstimate(
            flops=36 * 10**9, bytes_accessed=24 * 10**6, transcendentals=25 * 10**6
        ),
        name="layer",
    )(hidden, jnp.transpose(w_qkv, (1, 0, 2)), w_out, mods, gate, live)
    return jnp.where(here == chain - 1, entering, moved)


def solution(mesh):
    in_specs = (
        P("tm", None, "mp"),
        P(None, None, "mp"),
        P("mp", None),
        P(),
        P(),
        P(),
        P(None, None, "mp"),
    )
    out_specs = P("tm", None, "mp")
    return jax.shard_map(
        per_device, mesh=mesh, in_specs=in_specs, out_specs=out_specs, check_vma=False
    )
```

time: 425 us -> 178 us (0.42)
  waiting for transfers between devices: 205 us -> 0 us
  Pallas kernels: 0 us -> 167 us
  matrix products: 102 us -> 0 us
  local copies, waits for them, and re-layouts: 66 us -> 4.93 us
  other arithmetic: 23.2 us -> 5.39 us
  between operations: 15.4 us -> 0.06 us
  starting transfers between devices: 9.27 us -> 0 us
    pallas_call x0 -> x1, Pallas kernels: none -> 167 us  [per_device(): pl.pallas_call(functools.partial(kernel, chain), out_shape=jax.ShapeDtype...]
    ppermute x3 -> x0, waiting for transfers between devices: 93.5 us -> none  [the longest x1 55.6 us: with_halo(): after = lax.ppermute(initial, axis, down)]
    reduce_scatter x1 -> x0, waiting for transfers between devices: 64.7 us -> none  [per_device(): lax.psum_scatter(partial_terms.astype(jnp.bfloat16), 'mp', scatter_dimens...]
    dot_general x3 -> x0, matrix products: 62.4 us -> none  [the longest x1 33.9 us: per_device(): jnp.einsum('hqk,khd->qhd', weights, values, preferred_element_type=jnp.fl...]
    all_gather x1 -> x0, waiting for transfers between devices: 46.4 us -> none  [per_device(): whole = lax.all_gather(hidden, 'mp', axis=2, tiled=True)]
    sub x1 -> x0, matrix products: 39.6 us -> none  [per_device(): expd = jnp.exp(scores - top)]
    unnamed x11 -> x5, local copies, waits for them, and re-layouts: 19.6 us -> 0.05 us
    slice x5 -> x2, local copies, waits for them, and re-layouts: 13.4 us -> 0.63 us  [the longest x1 0.61 us: per_device(): gate = near[1, 2].reshape(4, 1, part)]
  transfers between devices with their start and end apart: 5 -> 0, of which waited for: 4 -> 0; matrix products, arithmetic and copies ran while one was open for 8% -> 0% of each run, Pallas kernels for 0% -> 0%
where the time goes in v1:
time: 178 us; the launch traced here: 177 us
  Pallas kernels  167 us (94%)
  other arithmetic  5.39 us (3%)
  local copies, waits for them, and re-layouts  4.93 us (3%)
    pallas_call x1, Pallas kernels, per_device(): pl.pallas_call(functools.partial(kernel, chain), out_shape=jax.ShapeDtype...  167 us

profile of v1, /device:TPU:1, one launch (start us, length us, event | category | flops | bytes accessed | tf_op | source)
XLA Modules:
  0.0 177.5 jit_solution(7135696386296366066)
XLA Ops:
  0.0 0.0 copy-start
  0.0 0.1 fusion
  0.1 1.4 fusion.3
  1.5 1.8 %or_convert_fusion = f32[8]{0:T(128)S(1)} fusion(pred[]{:T(512)S(6)} %lt.83, pred[]{:T(512)S(6)} %gt.3, s32[]{:T(128)} %bitcast.10, s32[]{:T(128)} %bitcast.9, s32[]{:T(128)} %bitcast.8), kind=kLoop, calls=%fused_computation.9 | loop fusion | flops 152 | bytes 46 | tf_op jit(solution)/shard_map/convert_element_type | solution.py:331
  3.3 0.7 broadcast_in_dim.2.live
  4.0 1.3 gather_fusion
  5.3 0.0 copy-done
  5.3 0.9 gather_fusion.1
  6.2 0.6 slice.18
  6.9 0.7 pad_maximum_fusion.mods
  7.6 0.0 copy-start.1
  7.6 167.1 %layer.1 = bf16[4,256,768]{2,1,0:T(8,128)(2,1)} custom-call(bf16[4,256,768]{2,1,0:T(8,128)(2,1)} %hid.1, bf16[3,3072,768]{2,1,0:T(8,128)(2,1)} %bitcast.15, bf16[768,3072]{1,0:T(8,128)(2,1)} %w_out.1, f32[3,2,3072]{2,1,0:T(2,128)} %pad_maximum_fusion.mods, f32[4,1,768]{2,1,0:T(1,128)} %bitcast.14, f32[8,128]{1,0:T(8,128)} %broadcast_in_dim.2.live), custom_call_target="tpu_custom_call" | custom-call | flops 35999997952 | bytes 24000000 | tf_op jit(solution)/shard_map/layer/pallas_call | solution.py:340
  174.8 0.0 copy-done.1
  174.8 2.7 %broadcast_select_fusion = bf16[4,256,768]{2,1,0:T(8,128)(2,1)} fusion(bf16[4,256,768]{2,1,0:T(8,128)(2,1)S(1)} %copy-done.1, bf16[4,256,768]{2,1,0:T(8,128)(2,1)} %layer.1, pred[]{:T(512)S(6)} %eq.3), kind=kLoop, calls=%fused_computation.2 | loop fusion | flops 786432 | bytes 4718593 | tf_op jit(solution)/shard_map/jit(_where)/select_n | solution.py:374
  (6 shorter events, 0.1 us)
Async XLA Ops:
  0.0 5.3 %copy-start = (f32[50,3,3072]{2,0,1:T(8,128)S(1)}, f32[50,3,3072]{2,0,1:T(8,128)}, u32[]{:S(2)}) copy-start(f32[50,3,3072]{2,0,1:T(8,128)} %param.10) | copy-start | bytes 5529604
  7.6 167.1 %copy-start.1 = (bf16[4,256,768]{2,1,0:T(8,128)(2,1)S(1)}, bf16[4,256,768]{2,1,0:T(8,128)(2,1)}, u32[]{:S(2)}) copy-start(bf16[4,256,768]{2,1,0:T(8,128)(2,1)} %param.13) | copy-start | bytes 4718596

commit v2 on v1

v2 whole, which is shorter than its diff:
```python
import functools

import jax
import jax.numpy as jnp
from jax import lax
from jax.experimental import pallas as pl
from jax.experimental.pallas import tpu as pltpu
from jax.sharding import PartitionSpec as P

HD = 64
HALO = 2
QUAD = 256
LN_ROWS = 32
PIECES = 4
MESH = pl.DeviceIdType.MESH

OWN_CORE, OWN_Y, OWN_FWD = 0, 4, 8
N_OWN, N_FWD, N_CORE_A, N_CORE_B = 12, 14, 16, 18
P_OWN, P_Y, P_CORE_A, P_CORE_B = 20, 22, 24, 26
TERM, PRE, FIN = 28, 36, 52
N_SEM = 68


def kernel(
    chain, hid, w, w_out, modulation, levels, counts, entering, out,
    x, wv, wo, shaped, qb, kb, vb, vlive, att, tsib, rsib, town, pre, rpre, fin,
    table, mods, gate, live, sums, mean_b, rstd_b, s_a, s_b, p_a, p_b, fade_a, fade_b, tops, acc, total,
    send_sem, recv_sem, w_sem, local_sem,
):
    c = lax.axis_index("tm")
    m = lax.axis_index("mp")
    sib, par, dia = m ^ 1, m ^ 2, m ^ 3
    up = lax.rem(c + 1, chain)
    down = lax.rem(c + chain - 1, chain)
    frames, tokens, part = hid.shape
    width = 4 * part
    heads_w = w.shape[2]
    keys = (frames + 2 * HALO) * tokens
    to_sib, to_par = (c, sib), (c, par)
    to_up, to_down = (up, par), (down, par)

    def rc(src, dst, s, dev):
        return pltpu.make_async_remote_copy(
            src_ref=src, dst_ref=dst, send_sem=send_sem.at[s], recv_sem=recv_sem.at[s],
            device_id=dev, device_id_type=MESH,
        )

    def arrived(dst, s):
        rc(dst, dst, s, to_sib).wait_recv()

    def w_copy(j):
        return pltpu.make_async_copy(
            w.at[j // 3, :, pl.ds((j % 3) * QUAD, QUAD)], wv.at[j], w_sem.at[j]
        )

    def wo_copy(g):
        return pltpu.make_async_copy(w_out.at[:, pl.ds(g * part, part)], wo.at[g], w_sem.at[9 + g])

    own_copy = pltpu.make_async_copy(hid, x.at[m, pl.ds(0, frames)], local_sem.at[0])
    last_copy = pltpu.make_async_copy(entering, out, local_sem.at[1])

    def mod_copy(kind):
        return pltpu.make_async_copy(modulation.at[kind], table, local_sem.at[2 + kind])

    mod_copy(0).start()
    own_copy.start()
    for j in range(9):
        w_copy(j).start()
    for g in range(4):
        wo_copy(g).start()

    barrier = pltpu.get_barrier_semaphore()
    for dev in (to_sib, to_par, to_up, to_down):
        pl.semaphore_signal(barrier, inc=1, device_id=dev, device_id_type=MESH)
    pl.semaphore_wait(barrier, 4)

    def own_core(i):
        return rc(hid.at[i], x.at[m, i], OWN_CORE + i, to_sib)

    def own_y(i):
        return rc(hid.at[i], x.at[m, i], OWN_Y + i, to_par)

    def own_fwd(i):
        return rc(x.at[par, i], x.at[par, i], OWN_FWD + i, to_sib)

    def n_own(i):
        return rc(hid.at[i], x.at[m, frames + HALO + i], N_OWN + i, to_down)

    def n_fwd(i):
        return rc(x.at[par, i], x.at[par, frames + HALO + i], N_FWD + i, to_down)

    def n_core_a(i):
        s = frames + HALO + i
        return rc(x.at[par, s], x.at[par, s], N_CORE_A + i, to_sib)

    def n_core_b(i):
        s = frames + HALO + i
        return rc(x.at[m, s], x.at[m, s], N_CORE_B + i, to_sib)

    def p_own(i):
        return rc(hid.at[frames - HALO + i], x.at[m, frames + i], P_OWN + i, to_up)

    def p_y(i):
        return rc(x.at[par, frames + i], x.at[par, frames + i], P_Y + i, to_par)

    def p_core_a(i):
        return rc(x.at[par, frames + i], x.at[par, frames + i], P_CORE_A + i, to_sib)

    def p_core_b(i):
        return rc(x.at[m, frames + i], x.at[m, frames + i], P_CORE_B + i, to_sib)

    for i in range(frames):
        own_y(i).start()
        own_core(i).start()
    n_own(0).start()
    p_own(0).start()
    p_own(1).start()

    @pl.when(c == chain - 1)
    def _():
        last_copy.start()

    before, after = jnp.maximum(c - 1, 0), jnp.minimum(c + 1, chain - 1)
    for i in range(frames + 2 * HALO):
        if i < frames:
            ok = i < counts[c]
        elif i < frames + HALO:
            ok = (c > 0) & (i - HALO < counts[before])
        else:
            ok = (c < chain - 1) & (i - HALO - frames < counts[after])
        row = jnp.where(ok, jnp.ones((1, 128), jnp.float32), jnp.zeros((1, 128), jnp.float32))
        live[i:i + 1, :] = row
        vlive[pl.ds(i * tokens, tokens), :] = jnp.broadcast_to(row, (tokens, 128)).astype(
            jnp.bfloat16
        )
    for kind in range(3):
        mod_copy(kind).wait()
        for n, near in enumerate((before, c, after)):
            row = table[pl.ds(levels[near], 1), :]
            if kind < 2:
                mods[n, kind] = jnp.broadcast_to(row + float(kind), (8, width))
            elif n == 1:
                for g in range(4):
                    gate[g] = row[:, g * part:(g + 1) * part]
        if kind < 2:
            mod_copy(kind + 1).start()
    own_copy.wait()

    def project(slot, span):
        def pieces(b):
            rows = pl.ds(pl.multiple_of(b * LN_ROWS, LN_ROWS), LN_ROWS)
            for f in range(4):
                for n in range(part // 128):
                    cols = slice(n * 128, (n + 1) * 128)
                    yield f, n, rows, x[f, slot, rows, cols].astype(jnp.float32)

        def add_up(b, carry):
            acc = [jnp.zeros((LN_ROWS, 128), jnp.float32)] * 2
            for f, n, rows, v in pieces(b):
                acc[n % 2] = acc[n % 2] + v
            sums[rows, :] = acc[0] + acc[1]
            return carry

        def add_squares(b, carry):
            acc = [jnp.zeros((LN_ROWS, 128), jnp.float32)] * 2
            for f, n, rows, v in pieces(b):
                d = v - mean_b[rows, :]
                acc[n % 2] = acc[n % 2] + d * d
            sums[rows, :] = acc[0] + acc[1]
            return carry

        def modulate(b, carry):
            for f, n, rows, v in pieces(b):
                cols = slice(f * part + n * 128, f * part + (n + 1) * 128)
                scale = jnp.concatenate([mods[span, 1, :, cols]] * (LN_ROWS // 8), axis=0)
                shift = jnp.concatenate([mods[span, 0, :, cols]] * (LN_ROWS // 8), axis=0)
                y = (v - mean_b[rows, :]) * rstd_b[rows, :] * scale + shift
                shaped[rows, cols] = y.astype(jnp.bfloat16)
            return carry

        steps = tokens // LN_ROWS
        lax.fori_loop(0, steps, add_up, 0)
        mean = jnp.sum(sums[...], axis=1, keepdims=True) * (1.0 / width)
        mean_b[...] = jnp.broadcast_to(mean, (tokens, 128))
        lax.fori_loop(0, steps, add_squares, 0)
        var = jnp.sum(sums[...], axis=1, keepdims=True) * (1.0 / width)
        rstd_b[...] = jnp.broadcast_to(lax.rsqrt(var + 1e-06), (tokens, 128))
        lax.fori_loop(0, steps, modulate, 0)
        lv = live[pl.ds(slot, 1), :]
        lv = jnp.concatenate([lv, lv], axis=1)
        rows = pl.ds(pl.multiple_of(slot * tokens, tokens), tokens)
        first = pl.ds(0, tokens)

        def tile(t, carry):
            k = jnp.dot(shaped[...], wv[3 + t], preferred_element_type=jnp.float32)
            kb[t, rows, :] = k.astype(jnp.bfloat16)
            k0 = kb[t, first, :].astype(jnp.float32)
            kb[t, rows, :] = jnp.where(lv > 0.5, k, k0).astype(jnp.bfloat16)
            v = jnp.dot(shaped[...], wv[6 + t], preferred_element_type=jnp.float32)
            vb[t, rows, :] = jnp.where(lv > 0.5, v, 0.0).astype(jnp.bfloat16)
            return carry

        lax.fori_loop(0, 3, tile, 0)

    def project_query(i):
        rows = pl.ds(pl.multiple_of(i * tokens, tokens), tokens)

        def tile(t, carry):
            q = jnp.dot(shaped[...], wv[t], preferred_element_type=jnp.float32)
            q = q.astype(jnp.bfloat16).astype(jnp.float32) * HD ** (-0.5)
            qb[t, rows, :] = q.astype(jnp.bfloat16)
            return carry

        lax.fori_loop(0, 3, tile, 0)

    for j in range(9):
        w_copy(j).wait()

    def own_step(i, carry):
        arrived(x.at[par, i], OWN_Y + i)
        own_fwd(i).start()

        @pl.when(i == 0)
        def _():
            n_fwd(0).start()
            n_own(1).start()

        @pl.when(i == 1)
        def _():
            n_fwd(1).start()

        @pl.when(i == 3)
        def _():
            arrived(x.at[par, frames], P_OWN)
            p_y(0).start()
            p_core_a(0).start()

        arrived(x.at[sib, i], OWN_CORE + i)
        arrived(x.at[dia, i], OWN_FWD + i)
        project(i, 1)
        project_query(i)
        return carry

    lax.fori_loop(0, frames, own_step, 0)
    arrived(x.at[par, frames + 1], P_OWN + 1)
    p_y(1).start()
    p_core_a(1).start()

    for g in range(4):
        wo_copy(g).wait()

    lane = lax.broadcasted_iota(jnp.int32, (1, 128), 1)
    low = lane < HD

    pairs = heads_w // 128
    early = 2 * pairs
    half = keys // 2

    def item(e):
        late = e - early
        b = late // pairs
        i = jnp.where(e < early, e // pairs, jnp.where(b < 2, b, b // 2 + 1))
        kh = jnp.where(e < early, 0, jnp.where(b < 2, 1, b % 2))
        return i, kh, e % pairs

    def place(e):
        i, kh, n = item(e)
        cols = pl.ds(pl.multiple_of((n % 2) * 128, 128), 128)
        return i, kh, n, n // 2, pl.ds(pl.multiple_of(kh * half, half), half), cols

    def score(e, s_ref):
        i, kh, n, t, key_rows, cols = place(e)
        q = qb[t, pl.ds(pl.multiple_of(i * tokens, tokens), tokens), cols]
        zero = jnp.zeros_like(q)
        q = jnp.concatenate([jnp.where(low, q, zero), jnp.where(low, zero, q)], axis=0)
        s_ref[...] = lax.dot_general(
            q, kb[t, key_rows, cols], (((1,), (1,)), ((), ())), preferred_element_type=jnp.float32
        )

    def weigh(e, s_ref, p_ref, fade):
        i, kh, n = item(e)
        for r in range(0, tokens, 32):
            rows = slice(r, r + 32)
            old = tops[i % 2, rows, :]
            new, fades = old, []
            for h in range(2):
                s = s_ref[h * tokens + r:h * tokens + r + 32, :]
                mine = lane == 2 * n + h
                was = jnp.max(jnp.where(mine & (kh > 0), old, -3e38), axis=1, keepdims=True)
                top = jnp.maximum(was, jnp.max(s, axis=1, keepdims=True))
                p_ref[h * tokens + r:h * tokens + r + 32, :] = jnp.exp(s - top).astype(jnp.bfloat16)
                new = jnp.where(mine, top, new)
                fades.append(jnp.exp(was - top))
            tops[i % 2, rows, :] = new
            fade[rows, :] = jnp.where(low, fades[0], fades[1])

    def mix(e, p_ref, fade):
        i, kh, n, t, key_rows, cols = place(e)
        v = jnp.concatenate([vb[t, key_rows, cols], vlive[key_rows, :]], axis=1)
        o = jnp.dot(p_ref[...], v, preferred_element_type=jnp.float32)
        z = jnp.where(low, o[:tokens, 128:], o[tokens:, 128:])
        o = jnp.where(low, o[:tokens, :128], o[tokens:, :128])
        later = jnp.broadcast_to(kh, (1, 128)) > 0
        o = jnp.where(later, acc[i % 2, n] * fade[...], 0.0) + o
        z = jnp.where(later, total[i % 2, n] * fade[...], 0.0) + z
        acc[i % 2, n] = o
        total[i % 2, n] = z
        att[i % 2, n] = (o / z).astype(jnp.bfloat16)

    def attend(e, end):
        score(e + 1, s_b)
        weigh(e, s_a, p_a, fade_a)
        mix(jnp.maximum(e - 1, 0), p_b, fade_b)
        score(jnp.minimum(e + 2, end - 1), s_a)
        weigh(e + 1, s_b, p_b, fade_b)
        mix(e, p_a, fade_a)

    def term(g, slot):
        a = jnp.concatenate([att[slot, n] for n in range(heads_w // 128)], axis=1)
        return jnp.dot(a, wo[g], preferred_element_type=jnp.float32).astype(jnp.bfloat16)

    def term_copy(i, b):
        return rc(tsib.at[b], rsib.at[i, b], TERM + 2 * i + b, to_sib)

    size = tokens // PIECES

    def piece(h):
        return pl.ds(pl.multiple_of(h * size, size), size)

    def pre_copy(i, h):
        return rc(
            pre.at[i % 2, piece(h)], rpre.at[i, piece(h)], PRE + PIECES * i + h, to_par
        )

    def fin_copy(i, h):
        return rc(
            fin.at[i % 2, piece(h)], out.at[i, piece(h)], FIN + PIECES * i + h, to_down
        )

    def frame_terms(i):
        slot = i % 2

        @pl.when(i >= 1)
        def _():
            term_copy(i - 1, 0).wait_send()
            term_copy(i - 1, 1).wait_send()

        tsib[0] = term(sib, slot)
        term_copy(i, 0).start()
        tsib[1] = term(dia, slot)
        term_copy(i, 1).start()
        town[slot, 0] = term(m, slot)
        town[slot, 1] = term(par, slot)

    def frame_pre(i):
        slot = i % 2

        @pl.when(i >= 2)
        def _():
            for h in range(PIECES):
                pre_copy(i - 2, h).wait_send()

        arrived(rsib.at[i, 0], TERM + 2 * i)
        for h in range(PIECES):
            rows = piece(h)
            pre[slot, rows] = (
                town[slot, 0, rows].astype(jnp.float32) + rsib[i, 0, rows].astype(jnp.float32)
            ).astype(jnp.bfloat16)
            pre_copy(i, h).start()

    def frame_fin(i, h):
        slot = i % 2
        rows = piece(h)

        @pl.when((i >= 2) & (c > 0))
        def _():
            fin_copy(i - 2, h).wait_send()

        @pl.when(h == 0)
        def _():
            arrived(rsib.at[i, 1], TERM + 2 * i + 1)

        arrived(rpre.at[i, rows], PRE + PIECES * i + h)
        mixed = (
            town[slot, 1, rows].astype(jnp.float32)
            + rsib[i, 1, rows].astype(jnp.float32)
            + rpre[i, rows].astype(jnp.float32)
        )
        res = x[par, i, rows].astype(jnp.float32) + gate[par] * mixed
        fin[slot, rows] = res.astype(jnp.bfloat16)

        @pl.when(c > 0)
        def _():
            fin_copy(i, h).start()

    def early_step(u, carry):
        attend(2 * u, early)

        @pl.when(u == pairs // 2)
        def _():
            arrived(x.at[par, frames + HALO], N_OWN)
            n_core_a(0).start()
            arrived(x.at[m, frames + HALO], N_FWD)
            n_core_b(0).start()

        return carry

    score(0, s_a)
    lax.fori_loop(0, pairs, early_step, 0)

    arrived(x.at[m, frames], P_Y)
    p_core_b(0).start()

    def halo_step(j, carry):
        slot = sum(jnp.where(j == n, s, 0) for n, s in enumerate((6, 4, 5, 7)))
        is_prev = slot < frames + HALO
        i = lax.rem(slot, 2)

        @pl.when(j == 2)
        def _():
            arrived(x.at[m, frames + 1], P_Y + 1)
            p_core_b(1).start()
            arrived(x.at[par, frames + HALO + 1], N_OWN + 1)
            n_core_a(1).start()
            arrived(x.at[m, frames + HALO + 1], N_FWD + 1)
            n_core_b(1).start()

        arrived(x.at[dia, slot], jnp.where(is_prev, P_CORE_A, N_CORE_A) + i)
        arrived(x.at[sib, slot], jnp.where(is_prev, P_CORE_B, N_CORE_B) + i)
        project(slot, jnp.where(is_prev, 0, 2))
        return carry

    lax.fori_loop(0, 2 * HALO, halo_step, 0)

    def late_step(u, carry):
        attend(early + 2 * u, items)

        @pl.when(u >= 8)
        def _():
            frame_fin((u - 8) // PIECES, (u - 8) % PIECES)

        @pl.when((u == 3) | (u == 6) | (u == 12))
        def _():
            frame_terms(jnp.where(u == 3, 0, jnp.where(u == 6, 1, 2)))

        @pl.when((u == 4) | (u == 7) | (u == 13))
        def _():
            frame_pre(jnp.where(u == 4, 0, jnp.where(u == 7, 1, 2)))

        return carry

    items = 2 * frames * pairs
    score(early, s_a)
    lax.fori_loop(0, (items - early) // 2, late_step, 0)
    mix(items - 1, p_b, fade_b)
    frame_terms(frames - 1)
    frame_pre(frames - 1)

    def last_step(q, carry):
        frame_fin(q // PIECES, q % PIECES)
        return carry

    lax.fori_loop((items - early) // 2 - 8, frames * PIECES, last_step, 0)

    for i in range(frames):
        own_y(i).wait_send()
        own_core(i).wait_send()
        own_fwd(i).wait_send()
    for i in range(HALO):
        for cp in (n_own, n_fwd, n_core_a, n_core_b, p_own, p_y, p_core_a, p_core_b):
            cp(i).wait_send()
    term_copy(frames - 1, 0).wait_send()
    term_copy(frames - 1, 1).wait_send()
    for i in range(frames - 2, frames):
        for h in range(PIECES):
            pre_copy(i, h).wait_send()

    @pl.when(c > 0)
    def _():
        for i in range(frames - 2, frames):
            for h in range(PIECES):
                fin_copy(i, h).wait_send()

    @pl.when(c < chain - 1)
    def _():
        for i in range(frames):
            for h in range(PIECES):
                arrived(out.at[i, piece(h)], FIN + PIECES * i + h)

    @pl.when(c == chain - 1)
    def _():
        last_copy.wait()


def per_device(hidden, w_qkv, w_out, modulation, levels, counts, entering):
    chain = lax.axis_size("tm")
    frames, tokens, part = hidden.shape
    model = w_qkv.shape[0]
    heads_w = w_qkv.shape[2]
    n_keys = (frames + 2 * HALO) * tokens
    bf, f32 = jnp.bfloat16, jnp.float32
    smem = pl.BlockSpec(memory_space=pltpu.SMEM)
    hbm = pl.BlockSpec(memory_space=pl.ANY)
    return pl.pallas_call(
        functools.partial(kernel, chain),
        out_shape=jax.ShapeDtypeStruct((frames, tokens, part), bf),
        in_specs=[hbm, hbm, hbm, hbm, smem, smem, hbm],
        out_specs=hbm,
        scratch_shapes=[
            pltpu.VMEM((4, frames + 2 * HALO, tokens, part), bf),
            pltpu.VMEM((9, model, QUAD), bf),
            pltpu.VMEM((4, heads_w, part), bf),
            pltpu.VMEM((tokens, model), bf),
            pltpu.VMEM((3, frames * tokens, QUAD), bf),
            pltpu.VMEM((3, n_keys, QUAD), bf),
            pltpu.VMEM((3, n_keys, QUAD), bf),
            pltpu.VMEM((n_keys, 128), bf),
            pltpu.VMEM((2, heads_w // 128, tokens, 128), bf),
            pltpu.VMEM((2, tokens, part), bf),
            pltpu.VMEM((frames, 2, tokens, part), bf),
            pltpu.VMEM((2, 2, tokens, part), bf),
            pltpu.VMEM((2, tokens, part), bf),
            pltpu.VMEM((frames, tokens, part), bf),
            pltpu.VMEM((2, tokens, part), bf),
            pltpu.VMEM(modulation.shape[::2], f32),
            pltpu.VMEM((3, 2, 8, model), f32),
            pltpu.VMEM((4, 1, part), f32),
            pltpu.VMEM((frames + 2 * HALO, 128), f32),
            pltpu.VMEM((tokens, 128), f32),
            pltpu.VMEM((tokens, 128), f32),
            pltpu.VMEM((tokens, 128), f32),
            pltpu.VMEM((2 * tokens, n_keys // 2), f32),
            pltpu.VMEM((2 * tokens, n_keys // 2), f32),
            pltpu.VMEM((2 * tokens, n_keys // 2), bf),
            pltpu.VMEM((2 * tokens, n_keys // 2), bf),
            pltpu.VMEM((tokens, 128), f32),
            pltpu.VMEM((tokens, 128), f32),
            pltpu.VMEM((2, tokens, 128), f32),
            pltpu.VMEM((2, heads_w // 128, tokens, 128), f32),
            pltpu.VMEM((2, heads_w // 128, tokens, 128), f32),
            pltpu.SemaphoreType.DMA((N_SEM,)),
            pltpu.SemaphoreType.DMA((N_SEM,)),
            pltpu.SemaphoreType.DMA((13,)),
            pltpu.SemaphoreType.DMA((5,)),
        ],
        compiler_params=pltpu.CompilerParams(
            collective_id=0, has_side_effects=True, vmem_limit_bytes=66 * 1000 * 1000
        ),
        cost_estimate=pl.CostEstimate(
            flops=36 * 10**9, bytes_accessed=24 * 10**6, transcendentals=25 * 10**6
        ),
        name="layer",
    )(
        hidden, jnp.transpose(w_qkv, (1, 0, 2)), w_out, jnp.transpose(modulation, (1, 0, 2)),
        levels, counts, entering,
    )


def solution(mesh):
    in_specs = (
        P("tm", None, "mp"),
        P(None, None, "mp"),
        P("mp", None),
        P(),
        P(),
        P(),
        P(None, None, "mp"),
    )
    out_specs = P("tm", None, "mp")
    return jax.shard_map(
        per_device, mesh=mesh, in_specs=in_specs, out_specs=out_specs, check_vma=False
    )
```

time: 178 us -> 150 us (0.84)
  Pallas kernels: 167 us -> 147 us
  other arithmetic: 5.39 us -> 0 us
  local copies, waits for them, and re-layouts: 4.93 us -> 2.65 us
    pallas_call x1, Pallas kernels: 167 us -> 147 us  [per_device(): pl.pallas_call(functools.partial(kernel, chain), out_shape=jax.ShapeDtype...]
    select_n x3 -> x0, other arithmetic: 2.81 us -> none  [the longest x1 2.72 us: per_device(): return jnp.where(here == chain - 1, entering, moved)]
    unnamed x5 -> x1, local copies, waits for them, and re-layouts: 0.05 us -> 2.65 us
    gather x2 -> x0, local copies, waits for them, and re-layouts: 2.18 us -> none  [per_device(): near = modulation[levels[jnp.stack([before, here, after])]]]
    convert_element_type x1 -> x0, other arithmetic: 1.83 us -> none  [per_device(): (prev_ok | own_ok | next_ok).astype(jnp.float32)[:, None]]
where the time goes in v2:
time: 150 us; the launch traced here: 149 us
  Pallas kernels  147 us (98%)
  local copies, waits for them, and re-layouts  2.65 us (2%)
    pallas_call x1, Pallas kernels, per_device(): pl.pallas_call(functools.partial(kernel, chain), out_shape=jax.ShapeDtype...  147 us

profile of v2, /device:TPU:1, one launch (start us, length us, event | category | flops | bytes accessed | tf_op | source)
XLA Modules:
  0.0 149.4 jit_solution(11055750382091931659)
XLA Ops:
  0.0 146.8 %layer.1 = bf16[4,256,768]{2,1,0:T(8,128)(2,1)} custom-call(bf16[4,256,768]{2,1,0:T(8,128)(2,1)} %hid.1, bf16[3,3072,768]{2,1,0:T(8,128)(2,1)} %bitcast.2, bf16[768,3072]{1,0:T(8,128)(2,1)} %w_out.1, f32[3,50,3072]{2,1,0:T(8,128)} %bitcast.3, s32[32]{0:T(128)} %levels.1, s32[32]{0:T(128)} %counts.1, bf16[4,256,768]{2,1,0:T(8,128)(2,1)} %entering.1), custom_call_target="tpu_custom_call" | custom-call | flops 35999997952 | bytes 24000000 | tf_op jit(solution)/shard_map/layer/pallas_call | solution.py:504
  146.8 2.7 %copy.9 = bf16[4,256,768]{2,1,0:T(8,128)(2,1)} copy(bf16[4,256,768]{2,1,0:T(8,128)(2,1)} %layer.1) | data formatting | bytes 3145728

commit v3 on v2

--- a/solution.py
+++ b/solution.py
@@ -38,6 +38,12 @@
     keys = (frames + 2 * HALO) * tokens
     to_sib, to_par = (c, sib), (c, par)
     to_up, to_down = (up, par), (down, par)
+    odd = lax.rem(c, 2)
+    even = odd == 0
+    near_first = HALO * (1 - odd)
+    far_first = HALO * odd
+    to_near = (c + 1 - 2 * odd, par)
+    to_far = (jnp.where(even, down, up), par)
 
     def rc(src, dst, s, dev):
         return pltpu.make_async_remote_copy(
@@ -84,10 +90,12 @@
         return rc(x.at[par, i], x.at[par, i], OWN_FWD + i, to_sib)
 
     def n_own(i):
-        return rc(hid.at[i], x.at[m, frames + HALO + i], N_OWN + i, to_down)
+        return rc(hid.at[near_first + i], x.at[m, frames + HALO + i], N_OWN + i, to_near)
 
     def n_fwd(i):
-        return rc(x.at[par, i], x.at[par, frames + HALO + i], N_FWD + i, to_down)
+        return rc(
+            x.at[par, near_first + i], x.at[par, frames + HALO + i], N_FWD + i, to_near
+        )
 
     def n_core_a(i):
         s = frames + HALO + i
@@ -98,7 +106,7 @@
         return rc(x.at[m, s], x.at[m, s], N_CORE_B + i, to_sib)
 
     def p_own(i):
-        return rc(hid.at[frames - HALO + i], x.at[m, frames + i], P_OWN + i, to_up)
+        return rc(hid.at[far_first + i], x.at[m, frames + i], P_OWN + i, to_far)
 
     def p_y(i):
         return rc(x.at[par, frames + i], x.at[par, frames + i], P_Y + i, to_par)
@@ -109,7 +117,8 @@
     def p_core_b(i):
         return rc(x.at[m, frames + i], x.at[m, frames + i], P_CORE_B + i, to_sib)
 
-    for i in range(frames):
+    for j in range(frames):
+        i = lax.rem(near_first + j, frames)
         own_y(i).start()
         own_core(i).start()
     n_own(0).start()
@@ -124,10 +133,12 @@
     for i in range(frames + 2 * HALO):
         if i < frames:
             ok = i < counts[c]
-        elif i < frames + HALO:
-            ok = (c > 0) & (i - HALO < counts[before])
         else:
-            ok = (c < chain - 1) & (i - HALO - frames < counts[after])
+            k = (i - frames) % HALO
+            prev_ok = (c > 0) & (frames - HALO + k < counts[before])
+            next_ok = (c < chain - 1) & (k < counts[after])
+            is_prev = even if i < frames + HALO else ~even
+            ok = (is_prev & prev_ok) | (~is_prev & next_ok)
         row = jnp.where(ok, jnp.ones((1, 128), jnp.float32), jnp.zeros((1, 128), jnp.float32))
         live[i:i + 1, :] = row
         vlive[pl.ds(i * tokens, tokens), :] = jnp.broadcast_to(row, (tokens, 128)).astype(
@@ -135,8 +146,8 @@
         )
     for kind in range(3):
         mod_copy(kind).wait()
-        for n, near in enumerate((before, c, after)):
-            row = table[pl.ds(levels[near], 1), :]
+        for n, who in enumerate((jnp.where(even, before, after), c, jnp.where(even, after, before))):
+            row = table[pl.ds(levels[who], 1), :]
             if kind < 2:
                 mods[n, kind] = jnp.broadcast_to(row + float(kind), (8, width))
             elif n == 1:
@@ -216,20 +227,21 @@
     for j in range(9):
         w_copy(j).wait()
 
-    def own_step(i, carry):
+    def own_step(j, carry):
+        i = lax.rem(near_first + j, frames)
         arrived(x.at[par, i], OWN_Y + i)
         own_fwd(i).start()
 
-        @pl.when(i == 0)
+        @pl.when(j == 0)
         def _():
             n_fwd(0).start()
             n_own(1).start()
 
-        @pl.when(i == 1)
+        @pl.when(j == 1)
         def _():
             n_fwd(1).start()
 
-        @pl.when(i == 3)
+        @pl.when(j == 3)
         def _():
             arrived(x.at[par, frames], P_OWN)
             p_y(0).start()
@@ -242,6 +254,11 @@
         return carry
 
     lax.fori_loop(0, frames, own_step, 0)
+    for i in range(HALO, frames):
+        lv = jnp.concatenate([live[i:i + 1, :]] * 2, axis=1)
+        for t in range(3):
+            rows = slice(i * tokens, (i + 1) * tokens)
+            kb[t, rows, :] = jnp.where(lv > 0.5, kb[t, rows, :], kb[t, :tokens, :])
     arrived(x.at[par, frames + 1], P_OWN + 1)
     p_y(1).start()
     p_core_a(1).start()

time: 150 us -> 140 us (0.933)
  Pallas kernels: 147 us -> 137 us
    pallas_call x1, Pallas kernels: 147 us -> 137 us  [per_device(): pl.pallas_call(functools.partial(kernel, chain), out_shape=jax.ShapeDtype...]
where the time goes in v3:
time: 140 us
  Pallas kernels  137 us (98%)
  local copies, waits for them, and re-layouts  2.65 us (2%)
    pallas_call x1, Pallas kernels, per_device(): pl.pallas_call(functools.partial(kernel, chain), out_shape=jax.ShapeDtype...  137 us

profile of v3, /device:TPU:1, one launch (start us, length us, event | category | flops | bytes accessed | tf_op | source)
XLA Modules:
  0.0 139.5 jit_solution(1295892540721453931)
XLA Ops:
  0.0 136.9 %layer.1 = bf16[4,256,768]{2,1,0:T(8,128)(2,1)} custom-call(bf16[4,256,768]{2,1,0:T(8,128)(2,1)} %hid.1, bf16[3,3072,768]{2,1,0:T(8,128)(2,1)} %bitcast.2, bf16[768,3072]{1,0:T(8,128)(2,1)} %w_out.1, f32[3,50,3072]{2,1,0:T(8,128)} %bitcast.3, s32[32]{0:T(128)} %levels.1, s32[32]{0:T(128)} %counts.1, bf16[4,256,768]{2,1,0:T(8,128)(2,1)} %entering.1), custom_call_target="tpu_custom_call" | custom-call | flops 35999997952 | bytes 24000000 | tf_op jit(solution)/shard_map/layer/pallas_call | solution.py:521
  136.9 2.7 %copy.9 = bf16[4,256,768]{2,1,0:T(8,128)(2,1)} copy(bf16[4,256,768]{2,1,0:T(8,128)(2,1)} %layer.1) | data formatting | bytes 3145728

commit v4 on v3

--- a/solution.py
+++ b/solution.py
@@ -70,11 +70,6 @@
 
     mod_copy(0).start()
     own_copy.start()
-    for j in range(9):
-        w_copy(j).start()
-    for g in range(4):
-        wo_copy(g).start()
-
     barrier = pltpu.get_barrier_semaphore()
     for dev in (to_sib, to_par, to_up, to_down):
         pl.semaphore_signal(barrier, inc=1, device_id=dev, device_id_type=MESH)
@@ -124,6 +119,10 @@
     n_own(0).start()
     p_own(0).start()
     p_own(1).start()
+    for j in range(9):
+        w_copy(j).start()
+    for g in range(4):
+        wo_copy(g).start()
 
     @pl.when(c == chain - 1)
     def _():

time: 140 us -> 140 us (level)
  no operation moved by 1% of the time
where the time goes in v4:
time: 140 us
  Pallas kernels  137 us (98%)
  local copies, waits for them, and re-layouts  2.65 us (2%)
    pallas_call x1, Pallas kernels, per_device(): pl.pallas_call(functools.partial(kernel, chain), out_shape=jax.ShapeDtype...  137 us

profile of v4, /device:TPU:1, one launch (start us, length us, event | category | flops | bytes accessed | tf_op | source)
XLA Modules:
  0.0 139.5 jit_solution(17448449053697049646)
XLA Ops:
  0.0 136.9 %layer.1 = bf16[4,256,768]{2,1,0:T(8,128)(2,1)} custom-call(bf16[4,256,768]{2,1,0:T(8,128)(2,1)} %hid.1, bf16[3,3072,768]{2,1,0:T(8,128)(2,1)} %bitcast.2, bf16[768,3072]{1,0:T(8,128)(2,1)} %w_out.1, f32[3,50,3072]{2,1,0:T(8,128)} %bitcast.3, s32[32]{0:T(128)} %levels.1, s32[32]{0:T(128)} %counts.1, bf16[4,256,768]{2,1,0:T(8,128)(2,1)} %entering.1), custom_call_target="tpu_custom_call" | custom-call | flops 35999997952 | bytes 24000000 | tf_op jit(solution)/shard_map/layer/pallas_call | solution.py:520
  136.9 2.7 %copy.9 = bf16[4,256,768]{2,1,0:T(8,128)(2,1)} copy(bf16[4,256,768]{2,1,0:T(8,128)(2,1)} %layer.1) | data formatting | bytes 3145728
